TPU v7x, 32 devices: a whole 2x2x4 slice. The times are simulated.
32 devices in a mesh: groups: 2 (over y), query: 4 (over x, core), ref: 4 (over z).
Axes of the slice: x: 2, y: 2, z: 4, core: 2. Of those that a mesh axis runs over, the one named last changes fastest.
Arguments:
- query_features: bfloat16 [64, 4096], P(None, ('groups', 'query', 'ref')), parts along dimension 1, may hold values from -6 to 6
- ref_features: bfloat16 [64, 65536], P(None, ('groups', 'ref', 'query')), parts along dimension 1, may hold values from -6 to 6
- query_blocks: int32 [64], P(('groups', 'query')), parts along dimension 0, may hold values from 0 to 7, as said below
- ref_blocks: int32 [1024], P(('groups', 'ref')), parts along dimension 0, may hold values from 0 to 7, as said below
- ref_labels: int32 [65536], P(('groups', 'ref')), parts along dimension 0, may hold values from 0 to 255
- cluster_pairs: int32 [48, 2], P('groups'), parts along dimension 0, may hold values from 0 to 7, as said below
Outputs:
- label_probs: float32 [4096, 256], P(('groups', 'query', 'ref')), parts along dimension 0
- query_potential: float32 [4096], P(('groups', 'query')), parts along dimension 0
- ref_potential: float32 [65536], P(('groups', 'ref')), parts along dimension 0
There are 2 independent parts, one for each index of `groups`. A program takes and returns all parts, laid end to end along the dimension named above; each array names one. Nothing has to cross between parts.
Inputs may be any that keep to these rules, and one draw needn't show every extreme that they name: `cluster_pairs`: every cluster is named as a query cluster by some pair and as a reference cluster by some pair. `query_blocks`: every cluster holds at least one block. `ref_blocks`: every cluster holds at least one block.
All inputs are finite; a program needn't handle non-finite values.
Results may differ from a plain program's by a relative error of at most 0.0013.
Values may be sent and summed in bfloat16 or wider, within the bound.
A program may use at most 128 MiB of HBM per device.

v0:
```python
import functools
import math

import jax
import jax.numpy as jnp
from jax import lax
from jax.experimental import pallas as pl
from jax.experimental.pallas import tpu as pltpu
from jax.sharding import PartitionSpec as P

PCA = 64
LABELS = 256
CB = 64
ITERS = 3
EPS = 0.002

SCALE = math.log2(math.e) / EPS
DOT_SCALE = 2.0 * SCALE / PCA
BLOCKED = -(2.0**100)
FLOOR = -1e20
TINY = 1e-37
DEPTH = 128
MESH = pl.DeviceIdType.MESH
F32 = jnp.float32
BF16 = jnp.bfloat16


def to_row(lanes, reduce):
    return reduce(lanes.T, axis=0, keepdims=True)


def from_row(row):
    return jnp.broadcast_to(row, (128, row.shape[1])).T


def kernel(
    nq, nr, q_ref, r_ref, labels_ref, qb_ref, rb_ref, pairs_ref,
    probs_ref, qpot_ref, rpot_ref,
    qg, aug_r, aug_q, scores, onehot, lanes, spread, peak, share, scale_row,
    rbuf, cbuf, lbuf, lsend,
    q_send, q_recv, r_send, r_recv, f_send, f_recv, row_send, row_recv, col_send, col_recv,
    l_send, l_recv,
):
    own_q = lax.axis_index("query")
    own_r = lax.axis_index("ref")
    qw = q_ref.shape[1]
    rw = r_ref.shape[1]
    rows_n = qw * nr
    cols_n = rw * nq
    chips = nq // 2
    core = lax.rem(own_q, 2)
    chip = own_q // 2
    sibling = chip * 2 + (1 - core)
    log_query = math.log2(rows_n * nq)
    log_ref = math.log2(cols_n * nr)

    barrier = pltpu.get_barrier_semaphore()
    for d in range(1, nq):
        pl.semaphore_signal(
            barrier, inc=1, device_id={"query": lax.rem(own_q + d, nq)}, device_id_type=MESH
        )
    for d in range(1, nr):
        pl.semaphore_signal(
            barrier, inc=1, device_id={"ref": lax.rem(own_r + d, nr)}, device_id_type=MESH
        )
    pl.semaphore_wait(barrier, nq + nr - 2)

    def block_cols(owner, width):
        return pl.ds(pl.multiple_of(owner * width, 128) if width % 128 == 0 else owner * width, width)

    own_cols = block_cols(own_r, qw)
    q_copies = []
    r_copies = []
    for d in range(1, chips):
        r_copies.append(
            pltpu.make_async_remote_copy(
                src_ref=r_ref,
                dst_ref=aug_r.at[pl.ds(0, PCA), block_cols(own_q, rw)],
                send_sem=r_send.at[d],
                recv_sem=r_recv.at[d],
                device_id={"query": lax.rem(chip + d, chips) * 2 + core},
                device_id_type=MESH,
            )
        )
        r_copies[-1].start()
    sibling_copy = pltpu.make_async_remote_copy(
        src_ref=r_ref,
        dst_ref=aug_r.at[pl.ds(0, PCA), block_cols(own_q, rw)],
        send_sem=r_send.at[0],
        recv_sem=r_recv.at[0],
        device_id={"query": sibling},
        device_id_type=MESH,
    )
    sibling_copy.start()
    for d in range(1, nr):
        q_copies.append(
            pltpu.make_async_remote_copy(
                src_ref=q_ref,
                dst_ref=qg.at[own_r],
                send_sem=q_send.at[d],
                recv_sem=q_recv.at[d],
                device_id={"ref": lax.rem(own_r + d, nr)},
                device_id_type=MESH,
            )
        )
        q_copies[-1].start()

    qg[own_r] = q_ref[...]
    aug_r[pl.ds(0, PCA), block_cols(own_q, rw)] = r_ref[...]
    aug_r[pl.ds(80, DEPTH - 80), :] = jnp.zeros((DEPTH - 80, cols_n), BF16)

    sub = lax.broadcasted_iota(jnp.int32, (8, 128), 0)
    lane = lax.broadcasted_iota(jnp.int32, (8, 128), 1)

    parts = []
    for k in range(rows_n // 128):
        cluster = jnp.where(lane < CB, qb_ref[0, 2 * k], qb_ref[0, 2 * k + 1])
        hit = jnp.zeros((8, 128), F32)
        for p in range(pairs_ref.shape[0]):
            both = jnp.logical_and(sub == pairs_ref[p, 1], cluster == pairs_ref[p, 0])
            hit = jnp.where(both, 1.0, hit)
        parts.append(jnp.where(hit > 0.5, 0.0, BLOCKED))
    blocked = jnp.concatenate(parts, axis=1)

    label_id = lax.broadcasted_iota(jnp.int32, (LABELS, 128), 0)

    def label_step(k, carry):
        cols = pl.ds(pl.multiple_of(k * 128, 128), 128)
        onehot[:, cols] = jnp.where(label_id == labels_ref[:, cols], 1.0, 0.0).astype(BF16)
        return carry

    lax.fori_loop(0, cols_n // 128, label_step, 0, unroll=2)

    for copy in q_copies:
        copy.wait()
    if qw % 128 == 0:
        q_cols = jnp.concatenate([qg[k].astype(F32) for k in range(nr)], axis=1)
    else:
        q_cols = jnp.concatenate([qg[k].astype(F32) for k in range(nr)], axis=1)
    q_norm = jnp.sum(q_cols * q_cols, axis=0, keepdims=True)
    filler = jnp.concatenate(
        [jnp.full((3, rows_n), -1.0, F32), jnp.zeros((DEPTH - PCA - 11, rows_n), F32)], axis=0
    )
    aug_q[...] = jnp.concatenate([q_cols, blocked, filler], axis=0).T.astype(BF16)

    lanes[...] = jnp.full((rows_n, 128), -3e38, F32)
    step_w = 256
    row_t = 128

    def score_block(owner):
        base = owner * rw

        def score_step(j, carry):
            cols = pl.ds(pl.multiple_of(base + j * step_w, 128), step_w)
            piece = aug_r[pl.ds(0, PCA), cols].astype(F32)
            half = 0.5 * jnp.sum(piece * piece, axis=0, keepdims=True)
            high = half.astype(BF16).astype(F32)
            middle = (half - high).astype(BF16).astype(F32)
            low = half - high - middle
            ids = []
            for t in range(step_w // 128):
                at = (base + j * step_w) // CB + 2 * t
                cluster = jnp.where(lane < CB, rb_ref[0, at], rb_ref[0, at + 1])
                ids.append(jnp.where(sub == cluster, 1.0, 0.0))
            extra = jnp.concatenate(
                [jnp.concatenate(ids, axis=1), high, middle, low, jnp.zeros((5, step_w), F32)],
                axis=0,
            )
            aug_r[pl.ds(PCA, 16), cols] = extra.astype(BF16)
            right = aug_r[:, cols]
            for i in range(rows_n // row_t):
                rows = pl.ds(i * row_t, row_t)
                value = DOT_SCALE * jnp.dot(aug_q[rows, :], right, preferred_element_type=F32)
                scores[rows, cols] = value
                top = lanes[rows, :]
                for t in range(step_w // 128):
                    top = jnp.maximum(top, value[:, t * 128 : (t + 1) * 128])
                lanes[rows, :] = top
            return carry

        lax.fori_loop(0, rw // step_w, score_step, 0)

    score_block(own_q)
    sibling_copy.wait()
    score_block(sibling)
    handed = []
    for d in range(1, chips):
        r_copies[d - 1].wait()
        owner = lax.rem(chip + chips - d, chips) * 2 + core
        block = aug_r.at[pl.ds(0, PCA), block_cols(owner, rw)]
        copy = pltpu.make_async_remote_copy(
            src_ref=block,
            dst_ref=block,
            send_sem=f_send.at[d],
            recv_sem=f_recv.at[d],
            device_id={"query": sibling},
            device_id_type=MESH,
        )
        copy.start()
        handed.append(copy)
    for d in range(1, chips):
        score_block(lax.rem(chip + chips - d, chips) * 2 + core)
    for d in range(1, chips):
        handed[d - 1].wait()
        score_block(lax.rem(chip + chips - d, chips) * 2 + 1 - core)

    def swap(buf, stage, send, recv, axis, own, count):
        copies = []
        for d in range(1, count):
            copies.append(
                pltpu.make_async_remote_copy(
                    src_ref=buf.at[stage, own],
                    dst_ref=buf.at[stage, own],
                    send_sem=send.at[stage, d],
                    recv_sem=recv.at[stage, d],
                    device_id={axis: lax.rem(own + d, count)},
                    device_id_type=MESH,
                )
            )
            copies[-1].start()
        return copies

    def swap_rows(stage, row):
        rbuf[stage, own_r] = row
        return swap(rbuf, stage, row_send, row_recv, "ref", own_r, nr)

    def swap_cols(stage, row):
        cbuf[stage, own_q] = row
        return swap(cbuf, stage, col_send, col_recv, "query", own_q, nq)

    def total_of(buf, stage, count):
        total = buf[stage, 0]
        for k in range(1, count):
            total = total + buf[stage, k]
        return total

    def joined(buf, stage, count):
        top = buf[stage, 0]
        for k in range(1, count):
            top = jnp.maximum(top, buf[stage, k])
        mass = jnp.exp2(buf[stage, 0] - top)
        for k in range(1, count):
            mass = mass + jnp.exp2(buf[stage, k] - top)
        return top, mass

    row_b = 64
    lane_steps = 8

    def row_sweep(term, bound):
        def over_rows(i, carry):
            rows = pl.ds(pl.multiple_of(i * row_b, row_b), row_b)
            held = bound[rows, :] if bound is not None else None

            def over_cols(j, acc):
                for t in range(lane_steps):
                    at = pl.multiple_of((j * lane_steps + t) * 128, 128)
                    acc = acc + term(rows, pl.ds(at, 128), held)
                return acc

            lanes[rows, :] = lax.fori_loop(
                0, cols_n // (128 * lane_steps), over_cols, jnp.zeros((row_b, 128), F32)
            )
            return carry

        lax.fori_loop(0, rows_n // row_b, over_rows, 0)
        return to_row(lanes[...], jnp.sum)

    top = jnp.maximum(to_row(lanes[...], jnp.max), FLOOR)
    spread[...] = from_row(top)
    mass = row_sweep(lambda rows, cols, held: jnp.exp2(scores[rows, cols] - held), spread)
    for copy in swap_rows(0, top + jnp.log2(jnp.maximum(mass, TINY))):
        copy.wait()
    top, mass = joined(rbuf, 0, nr)
    query_base = -log_query - (top + jnp.log2(mass))
    spread[...] = from_row(query_base)

    col_w = 256

    def column_first(j, carry):
        starts = [pl.multiple_of(j * col_w + t * 128, 128) for t in range(col_w // 128)]
        tops = [jnp.full((8, 128), FLOOR, F32) for _ in starts]
        for i in range(rows_n // row_b):
            rows = pl.ds(i * row_b, row_b)
            base = spread[rows, :]
            for t, at in enumerate(starts):
                value = scores[rows, pl.ds(at, 128)] + base
                tops[t] = jnp.maximum(
                    tops[t], jnp.max(value.reshape(row_b // 8, 8, 128), axis=0)
                )
        tops = [jnp.max(top, axis=0, keepdims=True) for top in tops]
        sums = [jnp.zeros((8, 128), F32) for _ in starts]
        for i in range(rows_n // row_b):
            rows = pl.ds(i * row_b, row_b)
            base = spread[rows, :]
            for t, at in enumerate(starts):
                value = jnp.exp2(scores[rows, pl.ds(at, 128)] + base - tops[t])
                scores[rows, pl.ds(at, 128)] = value
                sums[t] = sums[t] + jnp.sum(value.reshape(row_b // 8, 8, 128), axis=0)
        for t, at in enumerate(starts):
            peak[:, pl.ds(at, 128)] = tops[t]
            share[:, pl.ds(at, 128)] = jnp.sum(sums[t], axis=0, keepdims=True)
        return carry

    lax.fori_loop(0, cols_n // col_w, column_first, 0)
    for copy in swap_cols(0, peak[...] + jnp.log2(jnp.maximum(share[...], TINY))):
        copy.wait()
    top, mass = joined(cbuf, 0, nq)
    share[...] = jnp.exp2(peak[...] - top)
    peak[...] = top
    scale_row[...] = share[...] * (2.0**-log_ref) / mass

    for step in range(1, ITERS):
        part = row_sweep(lambda rows, cols, held: scores[rows, cols] * scale_row[:, cols], None)
        for copy in swap_rows(step, part):
            copy.wait()
        row_scale = 2.0**-log_query / total_of(rbuf, step, nr)
        spread[...] = from_row(row_scale)

        def column_later(j, carry):
            starts = [pl.multiple_of(j * col_w + t * 128, 128) for t in range(col_w // 128)]
            sums = [jnp.zeros((8, 128), F32) for _ in starts]
            for i in range(rows_n // row_b):
                rows = pl.ds(i * row_b, row_b)
                factor = spread[rows, :]
                for t, at in enumerate(starts):
                    value = scores[rows, pl.ds(at, 128)] * factor
                    sums[t] = sums[t] + jnp.sum(value.reshape(row_b // 8, 8, 128), axis=0)
            for t, at in enumerate(starts):
                scale_row[:, pl.ds(at, 128)] = jnp.sum(sums[t], axis=0, keepdims=True)
            return carry

        lax.fori_loop(0, cols_n // col_w, column_later, 0)
        for copy in swap_cols(step, share[...] * scale_row[...]):
            copy.wait()
        col_scale = 2.0**-log_ref / total_of(cbuf, step, nq)
        scale_row[...] = share[...] * col_scale

    plan_w = 512

    def label_mass(owner):
        rows = pl.ds(pl.multiple_of(owner * qw, qw), qw)
        factor = spread[rows, :]

        def over_cols(j, carry):
            acc, total = carry
            pieces = []
            for t in range(plan_w // 128):
                cols = pl.ds(pl.multiple_of(j * plan_w + t * 128, 128), 128)
                value = scores[rows, cols] * (factor * scale_row[:, cols])
                total = total + value
                pieces.append(value.astype(BF16))
            marks = onehot[:, pl.ds(pl.multiple_of(j * plan_w, 128), plan_w)]
            acc = acc + lax.dot_general(
                jnp.concatenate(pieces, axis=1),
                marks,
                (((1,), (1,)), ((), ())),
                preferred_element_type=F32,
            )
            return acc, total

        acc, total = lax.fori_loop(
            0,
            cols_n // plan_w,
            over_cols,
            (jnp.zeros((qw, LABELS), F32), jnp.zeros((qw, 128), F32)),
        )
        lanes[rows, :] = total
        return acc

    sent = []
    for d in range(1, nr):
        owner = lax.rem(own_r + d, nr)
        lsend[d] = label_mass(owner)
        copy = pltpu.make_async_remote_copy(
            src_ref=lsend.at[d],
            dst_ref=lbuf.at[d],
            send_sem=l_send.at[d],
            recv_sem=l_recv.at[d],
            device_id={"ref": owner},
            device_id_type=MESH,
        )
        copy.start()
        sent.append(copy)
    own_mass = label_mass(own_r)
    copies = swap_rows(ITERS, to_row(lanes[...], jnp.sum))
    qpot_ref[...] = (query_base + jnp.log2(row_scale)) * (1.0 / SCALE) + q_norm * (1.0 / PCA)
    rpot_ref[...] = (jnp.log2(col_scale) - peak[...]) * (1.0 / SCALE)
    for copy in copies:
        copy.wait()
    lanes[...] = from_row(1.0 / total_of(rbuf, ITERS, nr))
    for copy in sent:
        copy.wait()
    for d in range(1, nr):
        own_mass = own_mass + lbuf[d]
    inverse = lanes[pl.ds(pl.multiple_of(own_r * qw, qw), qw), :]
    for t in range(LABELS // 128):
        probs_ref[:, t * 128 : (t + 1) * 128] = own_mass[:, t * 128 : (t + 1) * 128] * inverse


def per_device(query_features, ref_features, query_blocks, ref_blocks, ref_labels, cluster_pairs):
    nq = lax.axis_size("query")
    nr = lax.axis_size("ref")
    qw = query_features.shape[1]
    rw = ref_features.shape[1]
    rows_n, cols_n = qw * nr, rw * nq
    dma = pltpu.SemaphoreType.DMA
    vmem = pl.BlockSpec(memory_space=pltpu.VMEM)
    smem = pl.BlockSpec(memory_space=pltpu.SMEM)
    probs, qpot, rpot = pl.pallas_call(
        functools.partial(kernel, nq, nr),
        out_shape=(
            jax.ShapeDtypeStruct((qw, LABELS), F32),
            jax.ShapeDtypeStruct((1, rows_n), F32),
            jax.ShapeDtypeStruct((1, cols_n), F32),
        ),
        in_specs=[vmem, vmem, vmem, smem, smem, smem],
        out_specs=(vmem, vmem, vmem),
        scratch_shapes=[
            pltpu.VMEM((nr, PCA, qw), BF16),
            pltpu.VMEM((DEPTH, cols_n), BF16),
            pltpu.VMEM((rows_n, DEPTH), BF16),
            pltpu.VMEM((rows_n, cols_n), F32),
            pltpu.VMEM((LABELS, cols_n), BF16),
            pltpu.VMEM((rows_n, 128), F32),
            pltpu.VMEM((rows_n, 128), F32),
            pltpu.VMEM((1, cols_n), F32),
            pltpu.VMEM((1, cols_n), F32),
            pltpu.VMEM((1, cols_n), F32),
            pltpu.VMEM((ITERS + 1, nr, 1, rows_n), F32),
            pltpu.VMEM((ITERS, nq, 1, cols_n), F32),
            pltpu.VMEM((nr, qw, LABELS), F32),
            pltpu.VMEM((nr, qw, LABELS), F32),
            dma((nr,)), dma((nr,)),
            dma((nq,)), dma((nq,)), dma((nq,)), dma((nq,)),
            dma((ITERS + 1, nr)), dma((ITERS + 1, nr)),
            dma((ITERS, nq)), dma((ITERS, nq)),
            dma((nr,)), dma((nr,)),
        ],
        compiler_params=pltpu.CompilerParams(
            collective_id=0, has_side_effects=True, vmem_limit_bytes=56 * 1024 * 1024
        ),
    )(
        query_features, ref_features, ref_labels.reshape(1, -1), query_blocks.reshape(1, -1),
        ref_blocks.reshape(1, -1), cluster_pairs,
    )
    return probs, qpot.reshape(-1), rpot.reshape(-1)


def solution(mesh):
    in_specs = (
        P(None, ("groups", "query", "ref")),
        P(None, ("groups", "ref", "query")),
        P(("groups", "query")),
        P(("groups", "ref")),
        P(("groups", "ref")),
        P("groups", None),
    )
    out_specs = (P(("groups", "query", "ref"), None), P(("groups", "query")), P(("groups", "ref")))
    return jax.shard_map(
        per_device, mesh=mesh, in_specs=in_specs, out_specs=out_specs, check_vma=False
    )
```

profile of v0, /device:TPU:0, one launch (start us, length us, event | category | flops | bytes accessed | tf_op | source)
XLA Modules:
  0.0 88.7 jit_solution(12189054837257029949)
XLA Ops:
  0.6 0.0 copy-start.2
  0.6 0.7 copy-done.2
  1.3 0.7 copy.9.pairs_ref
  2.0 83.9 %shard_map.85 = (f32[128,256]{1,0:T(8,128)}, f32[1,512]{1,0:T(1,128)}, f32[1,8192]{1,0:T(1,128)}) custom-call(bf16[64,128]{1,0:T(8,128)(2,1)} %q_ref.1, bf16[64,2048]{1,0:T(8,128)(2,1)} %r_ref.1, s32[1,8192]{1,0:T(1,128)} %bitcast.5, s32[1,8]{1,0:T(1,128)} %bitcast.8, s32[1,128]{1,0:T(1,128)} %bitcast.9, s32[24,2]{1,0:T(8,128)} %copy.9.pairs_ref), custom_call_target="tpu_custom_call" | custom-call | tf_op jit(solution)/shard_map/pallas_call | solution.py:409
  85.9 0.0 copy-start.1
  85.9 0.0 copy-start
  85.9 1.6 %copy.13 = f32[128,256]{1,0:T(8,128)} copy(f32[128,256]{1,0:T(8,128)} %get-tuple-element.12) | data formatting | bytes 262144
  87.5 0.0 copy-done.1
  87.5 0.6 copy.14
  88.1 0.0 copy-done
  88.1 0.6 copy.15
Async XLA Ops:
  0.6 0.7 copy-start.2
  85.9 1.6 %copy-start.1 = (f32[1,512]{1,0:T(1,128)S(1)}, f32[1,512]{1,0:T(1,128)}, u32[]{:S(2)}) copy-start(f32[1,512]{1,0:T(1,128)} %get-tuple-element.7) | copy-start | bytes 6148
  85.9 2.2 %copy-start = (f32[1,8192]{1,0:T(1,128)S(1)}, f32[1,8192]{1,0:T(1,128)}, u32[]{:S(2)}) copy-start(f32[1,8192]{1,0:T(1,128)} %get-tuple-element.8) | copy-start | bytes 98308
where the time goes:
time: 89 us; the launch traced here: 88.7 us
  Pallas kernels  83.9 us (94%)
  local copies, waits for them, and re-layouts  4.13 us (5%)
    pallas_call x1, Pallas kernels, per_device(): pl.pallas_call(functools.partial(kernel, nq, nr), out_shape=(jax.ShapeDty...  83.9 us
    unnamed x10, local copies, waits for them, and re-layouts  4.13 us

commit v1 on v0

--- a/solution.py
+++ b/solution.py
@@ -34,12 +34,13 @@
 
 
 def kernel(
-    nq, nr, q_ref, r_ref, labels_ref, qb_ref, rb_ref, pairs_ref,
-    probs_ref, qpot_ref, rpot_ref,
+    nq, nr, q_ref, r_ref, labels_in, qb_in, rb_in, pairs_in,
+    probs_out, qpot_out, rpot_out,
+    labels_ref, qb_ref, rb_ref, pairs_ref, probs_ref, qpot_ref, rpot_ref, partial, mass_sum,
     qg, aug_r, aug_q, scores, onehot, lanes, spread, peak, share, scale_row,
     rbuf, cbuf, lbuf, lsend,
     q_send, q_recv, r_send, r_recv, f_send, f_recv, row_send, row_recv, col_send, col_recv,
-    l_send, l_recv,
+    l_send, l_recv, in_sem, out_sem,
 ):
     own_q = lax.axis_index("query")
     own_r = lax.axis_index("ref")
@@ -54,6 +55,24 @@
     log_query = math.log2(rows_n * nq)
     log_ref = math.log2(cols_n * nr)
 
+    def block_cols(owner, width):
+        return pl.ds(pl.multiple_of(owner * width, 128), width)
+
+    fills = [
+        pltpu.make_async_copy(source, target, in_sem.at[k])
+        for k, (source, target) in enumerate(
+            [
+                (r_ref, aug_r.at[pl.ds(0, PCA), block_cols(own_q, rw)]),
+                (q_ref, qg.at[own_r]),
+                (labels_in, labels_ref),
+                (qb_in, qb_ref),
+                (rb_in, rb_ref),
+                (pairs_in, pairs_ref),
+            ]
+        )
+    ]
+    for fill in fills:
+        fill.start()
     barrier = pltpu.get_barrier_semaphore()
     for d in range(1, nq):
         pl.semaphore_signal(
@@ -65,29 +84,32 @@
         )
     pl.semaphore_wait(barrier, nq + nr - 2)
 
-    def block_cols(owner, width):
-        return pl.ds(pl.multiple_of(owner * width, 128) if width % 128 == 0 else owner * width, width)
-
-    own_cols = block_cols(own_r, qw)
+    half_w = rw // 2
     q_copies = []
-    r_copies = []
-    for d in range(1, chips):
-        r_copies.append(
-            pltpu.make_async_remote_copy(
-                src_ref=r_ref,
-                dst_ref=aug_r.at[pl.ds(0, PCA), block_cols(own_q, rw)],
-                send_sem=r_send.at[d],
-                recv_sem=r_recv.at[d],
+    r_copies = {}
+
+    def piece_of(owner, part):
+        return aug_r.at[
+            pl.ds(0, PCA), pl.ds(pl.multiple_of(owner * rw + part * half_w, 128), half_w)
+        ]
+
+    for part in range(2):
+        for d in range(1, chips):
+            copy = pltpu.make_async_remote_copy(
+                src_ref=r_ref.at[:, pl.ds(part * half_w, half_w)],
+                dst_ref=piece_of(own_q, part),
+                send_sem=r_send.at[part, d],
+                recv_sem=r_recv.at[part, d],
                 device_id={"query": lax.rem(chip + d, chips) * 2 + core},
                 device_id_type=MESH,
             )
-        )
-        r_copies[-1].start()
+            copy.start()
+            r_copies[part, d] = copy
     sibling_copy = pltpu.make_async_remote_copy(
         src_ref=r_ref,
         dst_ref=aug_r.at[pl.ds(0, PCA), block_cols(own_q, rw)],
-        send_sem=r_send.at[0],
-        recv_sem=r_recv.at[0],
+        send_sem=r_send.at[0, 0],
+        recv_sem=r_recv.at[0, 0],
         device_id={"query": sibling},
         device_id_type=MESH,
     )
@@ -105,10 +127,10 @@
         )
         q_copies[-1].start()
 
-    qg[own_r] = q_ref[...]
-    aug_r[pl.ds(0, PCA), block_cols(own_q, rw)] = r_ref[...]
     aug_r[pl.ds(80, DEPTH - 80), :] = jnp.zeros((DEPTH - 80, cols_n), BF16)
 
+    for fill in fills:
+        fill.wait()
     sub = lax.broadcasted_iota(jnp.int32, (8, 128), 0)
     lane = lax.broadcasted_iota(jnp.int32, (8, 128), 1)
 
@@ -116,8 +138,8 @@
     for k in range(rows_n // 128):
         cluster = jnp.where(lane < CB, qb_ref[0, 2 * k], qb_ref[0, 2 * k + 1])
         hit = jnp.zeros((8, 128), F32)
-        for p in range(pairs_ref.shape[0]):
-            both = jnp.logical_and(sub == pairs_ref[p, 1], cluster == pairs_ref[p, 0])
+        for p in range(pairs_ref.shape[1]):
+            both = jnp.logical_and(sub == pairs_ref[1, p], cluster == pairs_ref[0, p])
             hit = jnp.where(both, 1.0, hit)
         parts.append(jnp.where(hit > 0.5, 0.0, BLOCKED))
     blocked = jnp.concatenate(parts, axis=1)
@@ -133,10 +155,7 @@
 
     for copy in q_copies:
         copy.wait()
-    if qw % 128 == 0:
-        q_cols = jnp.concatenate([qg[k].astype(F32) for k in range(nr)], axis=1)
-    else:
-        q_cols = jnp.concatenate([qg[k].astype(F32) for k in range(nr)], axis=1)
+    q_cols = jnp.concatenate([qg[k].astype(F32) for k in range(nr)], axis=1)
     q_norm = jnp.sum(q_cols * q_cols, axis=0, keepdims=True)
     filler = jnp.concatenate(
         [jnp.full((3, rows_n), -1.0, F32), jnp.zeros((DEPTH - PCA - 11, rows_n), F32)], axis=0
@@ -147,8 +166,7 @@
     step_w = 256
     row_t = 128
 
-    def score_block(owner):
-        base = owner * rw
+    def score_block(base, width):
 
         def score_step(j, carry):
             cols = pl.ds(pl.multiple_of(base + j * step_w, 128), step_w)
@@ -178,31 +196,33 @@
                 lanes[rows, :] = top
             return carry
 
-        lax.fori_loop(0, rw // step_w, score_step, 0)
-
-    score_block(own_q)
+        lax.fori_loop(0, width // step_w, score_step, 0)
+
+    score_block(own_q * rw, rw)
     sibling_copy.wait()
-    score_block(sibling)
-    handed = []
-    for d in range(1, chips):
-        r_copies[d - 1].wait()
-        owner = lax.rem(chip + chips - d, chips) * 2 + core
-        block = aug_r.at[pl.ds(0, PCA), block_cols(owner, rw)]
-        copy = pltpu.make_async_remote_copy(
-            src_ref=block,
-            dst_ref=block,
-            send_sem=f_send.at[d],
-            recv_sem=f_recv.at[d],
-            device_id={"query": sibling},
-            device_id_type=MESH,
-        )
-        copy.start()
-        handed.append(copy)
-    for d in range(1, chips):
-        score_block(lax.rem(chip + chips - d, chips) * 2 + core)
-    for d in range(1, chips):
-        handed[d - 1].wait()
-        score_block(lax.rem(chip + chips - d, chips) * 2 + 1 - core)
+    score_block(sibling * rw, rw)
+    for part in range(2):
+        handed = []
+        for d in range(1, chips):
+            r_copies[part, d].wait()
+            block = piece_of(lax.rem(chip + chips - d, chips) * 2 + core, part)
+            copy = pltpu.make_async_remote_copy(
+                src_ref=block,
+                dst_ref=block,
+                send_sem=f_send.at[part, d],
+                recv_sem=f_recv.at[part, d],
+                device_id={"query": sibling},
+                device_id_type=MESH,
+            )
+            copy.start()
+            handed.append(copy)
+        for d in range(1, chips):
+            owner = lax.rem(chip + chips - d, chips) * 2 + core
+            score_block(owner * rw + part * half_w, half_w)
+        for d in range(1, chips):
+            handed[d - 1].wait()
+            owner = lax.rem(chip + chips - d, chips) * 2 + 1 - core
+            score_block(owner * rw + part * half_w, half_w)
 
     def swap(buf, stage, send, recv, axis, own, count):
         copies = []
@@ -274,10 +294,21 @@
     query_base = -log_query - (top + jnp.log2(mass))
     spread[...] = from_row(query_base)
 
-    col_w = 256
-
-    def column_first(j, carry):
-        starts = [pl.multiple_of(j * col_w + t * 128, 128) for t in range(col_w // 128)]
+    col_w = 512
+
+    def lane_starts(j):
+        return [pl.multiple_of(j * col_w + t * 128, 128) for t in range(col_w // 128)]
+
+    def squeeze(target, reduce):
+        def squeeze_step(j, carry):
+            for at in lane_starts(j):
+                target[:, pl.ds(at, 128)] = reduce(partial[:, pl.ds(at, 128)], axis=0, keepdims=True)
+            return carry
+
+        lax.fori_loop(0, cols_n // col_w, squeeze_step, 0, unroll=2)
+
+    def column_top(j, carry):
+        starts = lane_starts(j)
         tops = [jnp.full((8, 128), FLOOR, F32) for _ in starts]
         for i in range(rows_n // row_b):
             rows = pl.ds(i * row_b, row_b)
@@ -287,21 +318,30 @@
                 tops[t] = jnp.maximum(
                     tops[t], jnp.max(value.reshape(row_b // 8, 8, 128), axis=0)
                 )
-        tops = [jnp.max(top, axis=0, keepdims=True) for top in tops]
+        for t, at in enumerate(starts):
+            partial[:, pl.ds(at, 128)] = tops[t]
+        return carry
+
+    def column_first(j, carry):
+        starts = lane_starts(j)
+        tops = [jnp.broadcast_to(peak[:, pl.ds(at, 128)], (8, 128)) for at in starts]
         sums = [jnp.zeros((8, 128), F32) for _ in starts]
         for i in range(rows_n // row_b):
             rows = pl.ds(i * row_b, row_b)
-            base = spread[rows, :]
+            base = spread[rows, :].reshape(row_b // 8, 8, 128)
             for t, at in enumerate(starts):
-                value = jnp.exp2(scores[rows, pl.ds(at, 128)] + base - tops[t])
-                scores[rows, pl.ds(at, 128)] = value
-                sums[t] = sums[t] + jnp.sum(value.reshape(row_b // 8, 8, 128), axis=0)
+                value = scores[rows, pl.ds(at, 128)].reshape(row_b // 8, 8, 128)
+                value = jnp.exp2(value + base - tops[t][None])
+                scores[rows, pl.ds(at, 128)] = value.reshape(row_b, 128)
+                sums[t] = sums[t] + jnp.sum(value, axis=0)
         for t, at in enumerate(starts):
-            peak[:, pl.ds(at, 128)] = tops[t]
-            share[:, pl.ds(at, 128)] = jnp.sum(sums[t], axis=0, keepdims=True)
+            partial[:, pl.ds(at, 128)] = sums[t]
         return carry
 
+    lax.fori_loop(0, cols_n // col_w, column_top, 0)
+    squeeze(peak, jnp.max)
     lax.fori_loop(0, cols_n // col_w, column_first, 0)
+    squeeze(share, jnp.sum)
     for copy in swap_cols(0, peak[...] + jnp.log2(jnp.maximum(share[...], TINY))):
         copy.wait()
     top, mass = joined(cbuf, 0, nq)
@@ -317,7 +357,7 @@
         spread[...] = from_row(row_scale)
 
         def column_later(j, carry):
-            starts = [pl.multiple_of(j * col_w + t * 128, 128) for t in range(col_w // 128)]
+            starts = lane_starts(j)
             sums = [jnp.zeros((8, 128), F32) for _ in starts]
             for i in range(rows_n // row_b):
                 rows = pl.ds(i * row_b, row_b)
@@ -326,75 +366,97 @@
                     value = scores[rows, pl.ds(at, 128)] * factor
                     sums[t] = sums[t] + jnp.sum(value.reshape(row_b // 8, 8, 128), axis=0)
             for t, at in enumerate(starts):
-                scale_row[:, pl.ds(at, 128)] = jnp.sum(sums[t], axis=0, keepdims=True)
+                partial[:, pl.ds(at, 128)] = sums[t]
             return carry
 
         lax.fori_loop(0, cols_n // col_w, column_later, 0)
+        squeeze(scale_row, jnp.sum)
         for copy in swap_cols(step, share[...] * scale_row[...]):
             copy.wait()
         col_scale = 2.0**-log_ref / total_of(cbuf, step, nq)
         scale_row[...] = share[...] * col_scale
 
+    qpot_ref[...] = (query_base + jnp.log2(row_scale)) * (1.0 / SCALE) + q_norm * (1.0 / PCA)
+    rpot_ref[...] = (jnp.log2(col_scale) - peak[...]) * (1.0 / SCALE)
+    stores = [
+        pltpu.make_async_copy(qpot_ref, qpot_out, out_sem.at[0]),
+        pltpu.make_async_copy(rpot_ref, rpot_out, out_sem.at[1]),
+    ]
+    for store in stores:
+        store.start()
+
     plan_w = 512
-
-    def label_mass(owner):
-        rows = pl.ds(pl.multiple_of(owner * qw, qw), qw)
-        factor = spread[rows, :]
+    near = nr // 2
+    half_rows = qw * near
+    place = lax.rem(own_r, near)
+    near_base = own_r - place
+    far_base = lax.rem(near_base + near, nr)
+    lanes[...] = jnp.zeros_like(lanes)
+
+    def label_mass(base):
+        rows = pl.ds(pl.multiple_of(base * qw, half_rows), half_rows)
+        mass_sum[...] = jnp.zeros_like(mass_sum)
 
         def over_cols(j, carry):
-            acc, total = carry
             pieces = []
+            factor = spread[rows, :]
+            total = lanes[rows, :]
             for t in range(plan_w // 128):
                 cols = pl.ds(pl.multiple_of(j * plan_w + t * 128, 128), 128)
                 value = scores[rows, cols] * (factor * scale_row[:, cols])
                 total = total + value
                 pieces.append(value.astype(BF16))
+            lanes[rows, :] = total
             marks = onehot[:, pl.ds(pl.multiple_of(j * plan_w, 128), plan_w)]
-            acc = acc + lax.dot_general(
+            mass_sum[...] += lax.dot_general(
                 jnp.concatenate(pieces, axis=1),
                 marks,
                 (((1,), (1,)), ((), ())),
                 preferred_element_type=F32,
             )
-            return acc, total
-
-        acc, total = lax.fori_loop(
-            0,
-            cols_n // plan_w,
-            over_cols,
-            (jnp.zeros((qw, LABELS), F32), jnp.zeros((qw, 128), F32)),
-        )
-        lanes[rows, :] = total
-        return acc
+            return carry
+
+        lax.fori_loop(0, cols_n // plan_w, over_cols, 0)
 
     sent = []
-    for d in range(1, nr):
-        owner = lax.rem(own_r + d, nr)
-        lsend[d] = label_mass(owner)
+
+    def hand_out(base, slot, k):
+        at = lax.rem(place + k, near)
+        lsend[slot] = mass_sum[pl.ds(pl.multiple_of(at * qw, qw), qw), :].astype(BF16)
         copy = pltpu.make_async_remote_copy(
-            src_ref=lsend.at[d],
-            dst_ref=lbuf.at[d],
-            send_sem=l_send.at[d],
-            recv_sem=l_recv.at[d],
-            device_id={"ref": owner},
+            src_ref=lsend.at[slot],
+            dst_ref=lbuf.at[slot],
+            send_sem=l_send.at[slot],
+            recv_sem=l_recv.at[slot],
+            device_id={"ref": base + at},
             device_id_type=MESH,
         )
         copy.start()
         sent.append(copy)
-    own_mass = label_mass(own_r)
+
+    label_mass(far_base)
+    for k in range(near):
+        hand_out(far_base, near + k, k)
+    label_mass(near_base)
+    for k in range(1, near):
+        hand_out(near_base, k, k)
     copies = swap_rows(ITERS, to_row(lanes[...], jnp.sum))
-    qpot_ref[...] = (query_base + jnp.log2(row_scale)) * (1.0 / SCALE) + q_norm * (1.0 / PCA)
-    rpot_ref[...] = (jnp.log2(col_scale) - peak[...]) * (1.0 / SCALE)
+    own_mass = mass_sum[pl.ds(pl.multiple_of(place * qw, qw), qw), :]
     for copy in copies:
         copy.wait()
     lanes[...] = from_row(1.0 / total_of(rbuf, ITERS, nr))
-    for copy in sent:
+    for copy in reversed(sent):
         copy.wait()
     for d in range(1, nr):
-        own_mass = own_mass + lbuf[d]
+        own_mass = own_mass + lbuf[d].astype(F32)
     inverse = lanes[pl.ds(pl.multiple_of(own_r * qw, qw), qw), :]
     for t in range(LABELS // 128):
         probs_ref[:, t * 128 : (t + 1) * 128] = own_mass[:, t * 128 : (t + 1) * 128] * inverse
+    last = pltpu.make_async_copy(probs_ref, probs_out, out_sem.at[2])
+    last.start()
+    for store in stores:
+        store.wait()
+    last.wait()
 
 
 def per_device(query_features, ref_features, query_blocks, ref_blocks, ref_labels, cluster_pairs):
@@ -404,8 +466,8 @@
     rw = ref_features.shape[1]
     rows_n, cols_n = qw * nr, rw * nq
     dma = pltpu.SemaphoreType.DMA
-    vmem = pl.BlockSpec(memory_space=pltpu.VMEM)
-    smem = pl.BlockSpec(memory_space=pltpu.SMEM)
+    anywhere = pl.BlockSpec(memory_space=pl.ANY)
+    pairs_n = cluster_pairs.shape[0]
     probs, qpot, rpot = pl.pallas_call(
         functools.partial(kernel, nq, nr),
         out_shape=(
@@ -413,9 +475,18 @@
             jax.ShapeDtypeStruct((1, rows_n), F32),
             jax.ShapeDtypeStruct((1, cols_n), F32),
         ),
-        in_specs=[vmem, vmem, vmem, smem, smem, smem],
-        out_specs=(vmem, vmem, vmem),
+        in_specs=[anywhere] * 6,
+        out_specs=(anywhere, anywhere, anywhere),
         scratch_shapes=[
+            pltpu.VMEM((1, cols_n), jnp.int32),
+            pltpu.SMEM((1, query_blocks.shape[0]), jnp.int32),
+            pltpu.SMEM((1, ref_blocks.shape[0]), jnp.int32),
+            pltpu.SMEM((2, pairs_n), jnp.int32),
+            pltpu.VMEM((qw, LABELS), F32),
+            pltpu.VMEM((1, rows_n), F32),
+            pltpu.VMEM((1, cols_n), F32),
+            pltpu.VMEM((8, cols_n), F32),
+            pltpu.VMEM((rows_n // 2, LABELS), F32),
             pltpu.VMEM((nr, PCA, qw), BF16),
             pltpu.VMEM((DEPTH, cols_n), BF16),
             pltpu.VMEM((rows_n, DEPTH), BF16),
@@ -428,20 +499,20 @@
             pltpu.VMEM((1, cols_n), F32),
             pltpu.VMEM((ITERS + 1, nr, 1, rows_n), F32),
             pltpu.VMEM((ITERS, nq, 1, cols_n), F32),
-            pltpu.VMEM((nr, qw, LABELS), F32),
-            pltpu.VMEM((nr, qw, LABELS), F32),
+            pltpu.VMEM((nr, qw, LABELS), BF16),
+            pltpu.VMEM((nr, qw, LABELS), BF16),
             dma((nr,)), dma((nr,)),
-            dma((nq,)), dma((nq,)), dma((nq,)), dma((nq,)),
+            dma((2, nq)), dma((2, nq)), dma((2, nq)), dma((2, nq)),
             dma((ITERS + 1, nr)), dma((ITERS + 1, nr)),
             dma((ITERS, nq)), dma((ITERS, nq)),
-            dma((nr,)), dma((nr,)),
+            dma((nr,)), dma((nr,)), dma((6,)), dma((3,)),
         ],
         compiler_params=pltpu.CompilerParams(
             collective_id=0, has_side_effects=True, vmem_limit_bytes=56 * 1024 * 1024
         ),
     )(
         query_features, ref_features, ref_labels.reshape(1, -1), query_blocks.reshape(1, -1),
-        ref_blocks.reshape(1, -1), cluster_pairs,
+        ref_blocks.reshape(1, -1), cluster_pairs.T,
     )
     return probs, qpot.reshape(-1), rpot.reshape(-1)
 

time: 89 us -> 82.4 us (0.926)
  Pallas kernels: 83.9 us -> 78.8 us
  local copies, waits for them, and re-layouts: 4.13 us -> 2.78 us
    pallas_call x1, Pallas kernels: 83.9 us -> 78.8 us  [per_device(): pl.pallas_call(functools.partial(kernel, nq, nr), out_shape=(jax.ShapeDty...]
    unnamed x10 -> x7, local copies, waits for them, and re-layouts: 4.13 us -> 2.78 us
where the time goes in v1:
time: 82.4 us; the launch traced here: 82.2 us
  Pallas kernels  78.8 us (96%)
  local copies, waits for them, and re-layouts  2.78 us (3%)
    pallas_call x1, Pallas kernels, per_device(): pl.pallas_call(functools.partial(kernel, nq, nr), out_shape=(jax.ShapeDty...  78.8 us
    unnamed x7, local copies, waits for them, and re-layouts  2.78 us

profile of v1, /device:TPU:0, one launch (start us, length us, event | category | flops | bytes accessed | tf_op | source)
XLA Modules:
  0.0 82.2 jit_solution(6317635873825342811)
XLA Ops:
  0.6 78.8 %shard_map.85 = (f32[128,256]{1,0:T(8,128)}, f32[1,512]{1,0:T(1,128)}, f32[1,8192]{1,0:T(1,128)}) custom-call(bf16[64,128]{1,0:T(8,128)(2,1)} %q_ref.1, bf16[64,2048]{1,0:T(8,128)(2,1)} %r_ref.1, s32[1,8192]{1,0:T(1,128)} %bitcast.6, s32[1,8]{1,0:T(1,128)} %bitcast.10, s32[1,128]{1,0:T(1,128)} %bitcast.11, s32[2,24]{1,0:T(2,128)} %bitcast.9), custom_call_target="tpu_custom_call" | custom-call | tf_op jit(solution)/shard_map/pallas_call | solution.py:471
  79.5 0.0 copy-start.1
  79.5 0.0 copy-start
  79.5 1.6 %copy.12 = f32[128,256]{1,0:T(8,128)} copy(f32[128,256]{1,0:T(8,128)} %get-tuple-element.12) | data formatting | bytes 262144
  81.0 0.0 copy-done.1
  81.0 0.6 copy.13
  81.6 0.0 copy-done
  81.6 0.6 copy.14
Async XLA Ops:
  79.5 1.6 %copy-start.1 = (f32[1,512]{1,0:T(1,128)S(1)}, f32[1,512]{1,0:T(1,128)}, u32[]{:S(2)}) copy-start(f32[1,512]{1,0:T(1,128)} %get-tuple-element.7) | copy-start | bytes 6148
  79.5 2.2 %copy-start = (f32[1,8192]{1,0:T(1,128)S(1)}, f32[1,8192]{1,0:T(1,128)}, u32[]{:S(2)}) copy-start(f32[1,8192]{1,0:T(1,128)} %get-tuple-element.8) | copy-start | bytes 98308

commit v2 on v1

--- a/solution.py
+++ b/solution.py
@@ -36,7 +36,7 @@
 def kernel(
     nq, nr, q_ref, r_ref, labels_in, qb_in, rb_in, pairs_in,
     probs_out, qpot_out, rpot_out,
-    labels_ref, qb_ref, rb_ref, pairs_ref, probs_ref, qpot_ref, rpot_ref, partial, mass_sum,
+    labels_ref, qb_ref, rb_ref, pairs_ref, probs_ref, qpot_ref, rpot_ref, partial, mass_sum, ratios,
     qg, aug_r, aug_q, scores, onehot, lanes, spread, peak, share, scale_row,
     rbuf, cbuf, lbuf, lsend,
     q_send, q_recv, r_send, r_recv, f_send, f_recv, row_send, row_recv, col_send, col_recv,
@@ -332,7 +332,7 @@
             for t, at in enumerate(starts):
                 value = scores[rows, pl.ds(at, 128)].reshape(row_b // 8, 8, 128)
                 value = jnp.exp2(value + base - tops[t][None])
-                scores[rows, pl.ds(at, 128)] = value.reshape(row_b, 128)
+                ratios[rows, pl.ds(at, 128)] = value.reshape(row_b, 128)
                 sums[t] = sums[t] + jnp.sum(value, axis=0)
         for t, at in enumerate(starts):
             partial[:, pl.ds(at, 128)] = sums[t]
@@ -350,7 +350,7 @@
     scale_row[...] = share[...] * (2.0**-log_ref) / mass
 
     for step in range(1, ITERS):
-        part = row_sweep(lambda rows, cols, held: scores[rows, cols] * scale_row[:, cols], None)
+        part = row_sweep(lambda rows, cols, held: ratios[rows, cols] * scale_row[:, cols], None)
         for copy in swap_rows(step, part):
             copy.wait()
         row_scale = 2.0**-log_query / total_of(rbuf, step, nr)
@@ -363,7 +363,7 @@
                 rows = pl.ds(i * row_b, row_b)
                 factor = spread[rows, :]
                 for t, at in enumerate(starts):
-                    value = scores[rows, pl.ds(at, 128)] * factor
+                    value = ratios[rows, pl.ds(at, 128)] * factor
                     sums[t] = sums[t] + jnp.sum(value.reshape(row_b // 8, 8, 128), axis=0)
             for t, at in enumerate(starts):
                 partial[:, pl.ds(at, 128)] = sums[t]
@@ -403,7 +403,7 @@
             total = lanes[rows, :]
             for t in range(plan_w // 128):
                 cols = pl.ds(pl.multiple_of(j * plan_w + t * 128, 128), 128)
-                value = scores[rows, cols] * (factor * scale_row[:, cols])
+                value = ratios[rows, cols] * (factor * scale_row[:, cols])
                 total = total + value
                 pieces.append(value.astype(BF16))
             lanes[rows, :] = total
@@ -487,6 +487,7 @@
             pltpu.VMEM((1, cols_n), F32),
             pltpu.VMEM((8, cols_n), F32),
             pltpu.VMEM((rows_n // 2, LABELS), F32),
+            pltpu.VMEM((rows_n, cols_n), F32),
             pltpu.VMEM((nr, PCA, qw), BF16),
             pltpu.VMEM((DEPTH, cols_n), BF16),
             pltpu.VMEM((rows_n, DEPTH), BF16),

time: 82.4 us -> 78.1 us (0.948)
  Pallas kernels: 78.8 us -> 74.6 us
    pallas_call x1, Pallas kernels: 78.8 us -> 74.6 us  [per_device(): pl.pallas_call(functools.partial(kernel, nq, nr), out_shape=(jax.ShapeDty...]
where the time goes in v2:
time: 78.1 us; the launch traced here: 78 us
  Pallas kernels  74.6 us (96%)
  local copies, waits for them, and re-layouts  2.78 us (4%)
    pallas_call x1, Pallas kernels, per_device(): pl.pallas_call(functools.partial(kernel, nq, nr), out_shape=(jax.ShapeDty...  74.6 us
    unnamed x7, local copies, waits for them, and re-layouts  2.78 us

profile of v2, /device:TPU:0, one launch (start us, length us, event | category | flops | bytes accessed | tf_op | source)
XLA Modules:
  0.0 78.0 jit_solution(17710901253772932319)
XLA Ops:
  0.6 74.6 %shard_map.85 = (f32[128,256]{1,0:T(8,128)}, f32[1,512]{1,0:T(1,128)}, f32[1,8192]{1,0:T(1,128)}) custom-call(bf16[64,128]{1,0:T(8,128)(2,1)} %q_ref.1, bf16[64,2048]{1,0:T(8,128)(2,1)} %r_ref.1, s32[1,8192]{1,0:T(1,128)} %bitcast.6, s32[1,8]{1,0:T(1,128)} %bitcast.10, s32[1,128]{1,0:T(1,128)} %bitcast.11, s32[2,24]{1,0:T(2,128)} %bitcast.9), custom_call_target="tpu_custom_call" | custom-call | tf_op jit(solution)/shard_map/pallas_call | solution.py:471
  75.2 0.0 copy-start.1
  75.2 0.0 copy-start
  75.2 1.6 %copy.12 = f32[128,256]{1,0:T(8,128)} copy(f32[128,256]{1,0:T(8,128)} %get-tuple-element.12) | data formatting | bytes 262144
  76.8 0.0 copy-done.1
  76.8 0.6 copy.13
  77.4 0.0 copy-done
  77.4 0.6 copy.14
Async XLA Ops:
  75.2 1.6 %copy-start.1 = (f32[1,512]{1,0:T(1,128)S(1)}, f32[1,512]{1,0:T(1,128)}, u32[]{:S(2)}) copy-start(f32[1,512]{1,0:T(1,128)} %get-tuple-element.7) | copy-start | bytes 6148
  75.2 2.2 %copy-start = (f32[1,8192]{1,0:T(1,128)S(1)}, f32[1,8192]{1,0:T(1,128)}, u32[]{:S(2)}) copy-start(f32[1,8192]{1,0:T(1,128)} %get-tuple-element.8) | copy-start | bytes 98308

commit v3 on v2

--- a/solution.py
+++ b/solution.py
@@ -163,7 +163,7 @@
     aug_q[...] = jnp.concatenate([q_cols, blocked, filler], axis=0).T.astype(BF16)
 
     lanes[...] = jnp.full((rows_n, 128), -3e38, F32)
-    step_w = 256
+    step_w = 512
     row_t = 128
 
     def score_block(base, width):
@@ -385,7 +385,7 @@
     for store in stores:
         store.start()
 
-    plan_w = 512
+    plan_w = 2048
     near = nr // 2
     half_rows = qw * near
     place = lax.rem(own_r, near)

time: 78.1 us -> 73.6 us (0.942)
  Pallas kernels: 74.6 us -> 70 us
    pallas_call x1, Pallas kernels: 74.6 us -> 70 us  [per_device(): pl.pallas_call(functools.partial(kernel, nq, nr), out_shape=(jax.ShapeDty...]
where the time goes in v3:
time: 73.6 us; the launch traced here: 73.5 us
  Pallas kernels  70 us (95%)
  local copies, waits for them, and re-layouts  2.78 us (4%)
    pallas_call x1, Pallas kernels, per_device(): pl.pallas_call(functools.partial(kernel, nq, nr), out_shape=(jax.ShapeDty...  70 us
    unnamed x7, local copies, waits for them, and re-layouts  2.78 us

profile of v3, /device:TPU:0, one launch (start us, length us, event | category | flops | bytes accessed | tf_op | source)
XLA Modules:
  0.0 73.5 jit_solution(13383323610964565331)
XLA Ops:
  0.6 70.0 %shard_map.85 = (f32[128,256]{1,0:T(8,128)}, f32[1,512]{1,0:T(1,128)}, f32[1,8192]{1,0:T(1,128)}) custom-call(bf16[64,128]{1,0:T(8,128)(2,1)} %q_ref.1, bf16[64,2048]{1,0:T(8,128)(2,1)} %r_ref.1, s32[1,8192]{1,0:T(1,128)} %bitcast.6, s32[1,8]{1,0:T(1,128)} %bitcast.10, s32[1,128]{1,0:T(1,128)} %bitcast.11, s32[2,24]{1,0:T(2,128)} %bitcast.9), custom_call_target="tpu_custom_call" | custom-call | tf_op jit(solution)/shard_map/pallas_call | solution.py:471
  70.7 0.0 copy-start.1
  70.7 0.0 copy-start
  70.7 1.6 %copy.12 = f32[128,256]{1,0:T(8,128)} copy(f32[128,256]{1,0:T(8,128)} %get-tuple-element.12) | data formatting | bytes 262144
  72.3 0.0 copy-done.1
  72.3 0.6 copy.13
  72.8 0.0 copy-done
  72.9 0.6 copy.14
Async XLA Ops:
  70.7 1.6 %copy-start.1 = (f32[1,512]{1,0:T(1,128)S(1)}, f32[1,512]{1,0:T(1,128)}, u32[]{:S(2)}) copy-start(f32[1,512]{1,0:T(1,128)} %get-tuple-element.7) | copy-start | bytes 6148
  70.7 2.2 %copy-start = (f32[1,8192]{1,0:T(1,128)S(1)}, f32[1,8192]{1,0:T(1,128)}, u32[]{:S(2)}) copy-start(f32[1,8192]{1,0:T(1,128)} %get-tuple-element.8) | copy-start | bytes 98308
